TPU v7x, 32 devices: a whole 2x2x4 slice. The times are simulated.
32 devices in a mesh: parts: 32 (over z, y, x, core).
Axes of the slice: x: 2, y: 2, z: 4, core: 2. Of those that a mesh axis runs over, the one named last changes fastest.
Arguments:
- flow_state: float32 [5, 64, 2048], P(None, None, 'parts'), may hold values from -2 to 14, as said below
- state_tangent: float32 [5, 64, 2048], P(None, None, 'parts'), may hold values from -6 to 6
- far_field: float32 [5], replicated, may hold values from -0.3 to 5, as said below
- coordinates: float32 [3, 3264], P(None, 'parts'), as said below
- damping: float32 [2], replicated, may hold values from 0.1 to 1
- face_neighbour: int32 [6, 2048], P(None, 'parts'), may hold values from 0 to 96, as said below
- element_nodes: int32 [8, 2048], P(None, 'parts'), may hold values from 0 to 152, as said below
- upper_sends: int32 [1024], P('parts'), may hold values from 0 to 63, as said below
- lower_sends: int32 [1024], P('parts'), may hold values from 0 to 63, as said below
- node_sends: int32 [1632], P('parts'), may hold values from 0 to 101, as said below
- shock_flags: int32 [2048], P('parts'), may hold values from 0 to 1, as said below
Outputs:
- residual: float32 [5, 64, 2048], P(None, None, 'parts')
- state_change: float32 [5, 64, 2048], P(None, None, 'parts')
- node_update: float32 [3, 3264], P(None, 'parts')
Inputs may be any that keep to these rules, and one draw needn't show every extreme that they name: `flow_state`: density and pressure at each point lie in 0.5 to 2 and velocity components within 1 of (0, 0, 1.5). `far_field`: density and pressure lie in 0.8 to 1.2, velocity components within 0.2 of (0, 0, 1.5). `coordinates`: hexahedra stay valid: each element's trilinear map keeps a positive Jacobian at all points. `face_neighbour`: entry f of an element is a local element below 64, 64 + a halo slot below 32 (faces 0 and 1 only), or 96 for the far field; neighbours share the element's reference orientation. `element_nodes`: a local owned node below 102, or 102 + a halo slot of a node owned by the next partition. `upper_sends`: on each partition 32 distinct local elements. `lower_sends`: on each partition 32 distinct local elements. `node_sends`: on each partition 51 distinct owned nodes. `shock_flags`: at most 16 flagged elements in one partition, and some partition has exactly 16.
All inputs are finite; a program needn't handle non-finite values.
Results may differ from a plain program's by a relative error of at most 0.0003.
Values sent between devices are 32-bit elements; how exact they have to be, the bound alone decides.
A program may use at most 128 MiB of HBM per device.

v0:
```python
import functools
import math

import jax
import jax.numpy as jnp
import ml_dtypes
import numpy as np
from jax import lax
from jax.experimental import pallas as pl
from jax.experimental.pallas import tpu as pltpu
from jax.sharding import PartitionSpec as P

SOFT = 0.01
MESH = pl.DeviceIdType.MESH
F32 = jnp.float32
BF16 = jnp.bfloat16
OTHER = 4096
INPUTS = 16
VMEM_LIMIT = 60 * 1024 * 1024
LOAD_ORDER = (9, 3, 7, 8, 0, 1, 11, 5, 6, 14, 2, 4, 10, 12, 13, 15)
LANES = 128
FACE = 16
POINTS = 64


def lobatto_tables():
    points = np.array([-1.0, -math.sqrt(0.2), math.sqrt(0.2), 1.0])
    weights = np.array([1.0, 5.0, 5.0, 1.0]) / 6.0
    derivative = np.zeros((4, 4))
    for a in range(4):
        for b in range(4):
            if a == b:
                derivative[a, b] = sum((1.0 / (points[a] - points[m]) for m in range(4) if m != a))
            else:
                numerator = 1.0
                denominator = 1.0
                for m in range(4):
                    if m != b:
                        denominator *= points[b] - points[m]
                        if m != a:
                            numerator *= points[a] - points[m]
                derivative[a, b] = numerator / denominator
    return (points, weights, derivative)


def shape_gradients():
    points = lobatto_tables()[0]
    gradients = np.zeros((3, 64, 8))
    for q in range(64):
        position = (q // 16, q // 4 % 4, q % 4)
        for k in range(8):
            corner_bits = (k // 4, k // 2 % 2, k % 2)
            for j in range(3):
                factor = 1.0
                for m in range(3):
                    orient = 1.0 if corner_bits[m] == 1 else -1.0
                    if m == j:
                        factor *= 0.5 * orient
                    else:
                        factor *= 0.5 * (1.0 + orient * points[position[m]])
                gradients[j, q, k] = factor
    return gradients


def edge_laplacian():
    matrix = np.zeros((8, 8))
    for k in range(8):
        matrix[k, k] = 3.0
        for b in range(3):
            matrix[k, k ^ 1 << b] = -1.0
    return matrix


def tables():
    _, weights, derivative = lobatto_tables()
    gradients = shape_gradients()
    grid = np.arange(64).reshape(4, 4, 4)
    face_rows = [np.take(grid, 3 * (f % 2), axis=f // 2).reshape(-1) for f in range(6)]
    select = np.zeros((96, 64))
    select[np.arange(96), np.concatenate(face_rows)] = 1.0
    volume = (weights[:, None, None] * weights[None, :, None] * weights[None, None, :]).reshape(-1)
    face_weights = np.tile((weights[:, None] * weights[None, :]).reshape(-1), 6)
    eye = np.eye(4)
    applied = [
        np.kron(derivative, np.kron(eye, eye)),
        np.kron(eye, np.kron(derivative, eye)),
        np.kron(eye, np.kron(eye, derivative)),
    ]
    assembly = np.concatenate(
        [volume[:, None] * m for m in applied] + [select.T * face_weights[None, :]], axis=1
    )
    first = [gradients[(f // 2 + 1) % 3][face_rows[f]] * (2.0 * (f % 2) - 1.0) for f in range(6)]
    second = [gradients[(f // 2 + 2) % 3][face_rows[f]] for f in range(6)]
    tangents = np.concatenate([gradients.reshape(192, 8)] + first + second, axis=0)
    hi, mid, lo = split_table(np.concatenate([tangents, edge_laplacian()], axis=0))
    arrays = (
        np.concatenate([select] * 3, axis=1),
        two_parts(assembly),
        two_parts(assembly.T),
        np.concatenate([hi, hi, hi, mid, mid, lo], axis=1),
        two_parts(tangents.T),
    )
    return [np.ascontiguousarray(a, dtype=np.float32) for a in arrays]


def split_table(a):
    parts, rest = [], a
    for _ in range(3):
        part = rest.astype(ml_dtypes.bfloat16).astype(np.float64)
        parts.append(part)
        rest = rest - part
    return parts


def two_parts(a):
    hi, mid, _ = split_table(a)
    return np.concatenate([hi, mid, hi], axis=1)


def split(x, count):
    parts = []
    for _ in range(count - 1):
        part = x.astype(BF16).astype(F32)
        parts.append(part)
        x = x - part
    return parts + [x]


def rows_of(parts):
    return jnp.concatenate(parts, axis=0).astype(BF16)


def apply_table(table, data):
    hi, lo = split(data, 2)
    return jnp.dot(table, rows_of([hi, hi, lo]), preferred_element_type=F32)


def pick(data, hot):
    count = data.shape[0]
    out = jnp.dot(rows_of(split(data, 3)), hot, preferred_element_type=F32)
    return out[:count] + out[count:2 * count] + out[2 * count:]


def pick_t(data, hot):
    count = data.shape[0]
    out = lax.dot_general(
        rows_of(split(data, 3)), hot, (((1,), (1,)), ((), ())), preferred_element_type=F32
    )
    return out[:count] + out[count:2 * count] + out[2 * count:]


def cross(a, b):
    return [
        a[1] * b[2] - a[2] * b[1],
        a[2] * b[0] - a[0] * b[2],
        a[0] * b[1] - a[1] * b[0],
    ]


def dot3(a, b):
    return a[0] * b[0] + a[1] * b[1] + a[2] * b[2]


class Gas:
    def __init__(self, values):
        self.u, self.m = values, values[1:4]
        self.inv = 1.0 / values[0]
        self.v = [m * self.inv for m in self.m]
        self.p = 0.4 * (values[4] - 0.5 * dot3(self.m, self.v))
        self.h = values[4] + self.p

    def vary(self, tangent):
        self.du, self.dm = tangent, tangent[1:4]
        self.dv = [(self.dm[i] - self.v[i] * tangent[0]) * self.inv for i in range(3)]
        self.dp = 0.4 * (tangent[4] - 0.5 * (dot3(self.dm, self.v) + dot3(self.m, self.dv)))
        self.dh = tangent[4] + self.dp

    def along(self, n):
        vn = dot3(self.v, n)
        return [dot3(self.m, n)] + [self.m[k] * vn + self.p * n[k] for k in range(3)] + [self.h * vn]

    def along_change(self, n):
        vn, dvn = dot3(self.v, n), dot3(self.dv, n)
        middle = [self.dm[k] * vn + self.m[k] * dvn + self.dp * n[k] for k in range(3)]
        return [dot3(self.dm, n)] + middle + [self.dh * vn + self.h * dvn]

    def against(self, y):
        common = y[1] * self.m[0] + y[2] * self.m[1] + y[3] * self.m[2] + y[4] * self.h
        return [y[0] * self.m[i] + self.v[i] * common + y[1 + i] * self.p for i in range(3)]

    def speed(self, n, square, size):
        a = dot3(self.v, n)
        root = jnp.sqrt(a * a + SOFT * square)
        self.sound = jnp.sqrt(1.4 * self.p * self.inv)
        inv_root = 1.0 / root
        self.slope = a * inv_root
        sn = SOFT * inv_root + self.sound / size
        return root + self.sound * size, [self.slope * self.v[i] + sn * n[i] for i in range(3)]

    def speed_change(self, n, size):
        dsound = 0.7 * (self.dp - self.p * self.du[0] * self.inv) * self.inv / self.sound
        return self.slope * dot3(self.dv, n) + dsound * size


def kernel(n, group, *refs):
    sources, refs = refs[:INPUTS], refs[INPUTS:]
    results, refs = refs[:3], refs[3:]
    held, refs = refs[:INPUTS], refs[INPUTS:]
    (res_ref, change_ref, update_ref), refs = refs[:3], refs[3:]
    (state_ref, tangent_ref, far_ref, place_ref, damp_ref, neigh_ref, nodes_ref, upper_ref, lower_ref,
     sends_ref, flag_ref, select_ref, asm_ref, asm_t_ref, geo_ref, geo_t_ref) = held
    (up_out, up_in, down_out, down_in, place_out, place_in,
     gup_out, gup_in, gdown_out, gdown_in, sum_out, sum_in, send_sem, recv_sem, load_sem) = refs
    loads = [
        pltpu.make_async_copy(sources[i], held[i], load_sem.at[i]) for i in range(INPUTS)
    ]
    stores = [
        pltpu.make_async_copy(source, results[i], load_sem.at[INPUTS + i])
        for i, source in enumerate((res_ref, change_ref, update_ref))
    ]
    for i in LOAD_ORDER:
        loads[i].start()
    me = lax.axis_index("parts")
    right, left = lax.rem(me + 1, n), lax.rem(me + n - 1, n)
    elements = state_ref.shape[2]
    slots = upper_ref.shape[1]
    owned = place_ref.shape[1]
    shared = sends_ref.shape[1]
    own_pad = -(-owned // LANES) * LANES
    halo_pad = -(-shared // LANES) * LANES
    wide = 2 * elements

    stages = []
    low = 1
    while low < n:
        size = min(group, n // low)
        stages.append([low * k for k in range(1, size)])
        low *= size
    masks = [m for stage in stages for m in stage]

    def partner(mask):
        bit = me // mask % 2 if mask & (mask - 1) == 0 else None
        if bit is not None:
            return me + mask * (1 - 2 * bit)
        result = me
        b = 1
        while b <= mask:
            if mask & b:
                result = result + b * (1 - 2 * (me // b % 2))
            b *= 2
        return result

    partners = [partner(m) for m in masks]

    def remote(index, src, dst, device):
        return pltpu.make_async_remote_copy(
            src_ref=src, dst_ref=dst, send_sem=send_sem.at[index], recv_sem=recv_sem.at[index],
            device_id=(device,), device_id_type=MESH,
        )

    barrier = pltpu.get_barrier_semaphore()
    for device in [left, right] + partners:
        pl.semaphore_signal(barrier, inc=1, device_id=(device,), device_id_type=MESH)

    for i in LOAD_ORDER[:6]:
        loads[i].wait()
    own_rows = lax.broadcasted_iota(jnp.int32, (own_pad, halo_pad), 0)
    sends = sends_ref[...]
    if halo_pad > shared:
        sends = jnp.concatenate([sends, jnp.full((1, halo_pad - shared), -1, jnp.int32)], axis=1)
    sent_nodes = jnp.where(own_rows == sends, 1.0, 0.0).astype(BF16)
    places = jnp.zeros((8, own_pad), F32)
    place = place_ref[...]
    if own_pad > owned:
        place = jnp.concatenate([place, jnp.zeros((3, own_pad - owned), F32)], axis=1)
    places = jnp.concatenate([place, jnp.zeros((5, own_pad), F32)], axis=0)
    place_out[...] = pick(places, sent_nodes)

    row = lax.broadcasted_iota(jnp.int32, (wide, wide), 0)
    in_tangent = row >= elements
    local_key = jnp.where(in_tangent, row - elements + OTHER, row)
    slot = jnp.where(in_tangent, row - elements, row)
    halo_key = jnp.where(slot < slots, local_key + elements, -1)

    def one_hot(key, index):
        return jnp.where(key == index, 1.0, 0.0).astype(BF16)

    def send_hot(index):
        if slots < elements:
            pad = jnp.full((1, elements - slots), -2, jnp.int32)
            index = jnp.concatenate([index, pad, index + OTHER, pad], axis=1)
        else:
            index = jnp.concatenate([index, index + OTHER], axis=1)
        return one_hot(local_key, index)

    values = [state_ref[v] for v in range(5)]
    tangent = [tangent_ref[v] for v in range(5)]
    both = [jnp.concatenate([values[v], tangent[v]], axis=1) for v in range(5)]
    top = POINTS - FACE
    up_out[...] = pick(
        jnp.concatenate([both[v][top:POINTS] for v in range(5)], axis=0), send_hot(upper_ref[...])
    )
    down_out[...] = pick(
        jnp.concatenate([both[v][0:FACE] for v in range(5)], axis=0), send_hot(lower_ref[...])
    )
    pl.semaphore_wait(barrier, 2 + len(partners))
    place_copy = remote(0, place_out, place_in, left)
    up_copy = remote(1, up_out, up_in, right)
    down_copy = remote(2, down_out, down_in, left)
    place_copy.start()
    up_copy.start()
    down_copy.start()

    for i in LOAD_ORDER[6:]:
        loads[i].wait()
    weight = flag_ref[...].astype(F32)
    far_field = far_ref[...]
    damping = damp_ref[...]
    gas = Gas(values)
    select = select_ref[...].astype(BF16)
    traces = jnp.dot(
        select, rows_of(split(jnp.concatenate(both, axis=1), 3)), preferred_element_type=F32
    )
    trace = [traces[:, v * wide:(v + 1) * wide] for v in range(5)]
    neigh = neigh_ref[...]
    neigh = jnp.concatenate([neigh, neigh + OTHER], axis=1)
    far = jnp.where(neigh == elements + slots, 1.0, 0.0).astype(F32)
    outer = []
    for f in range(6):
        opposite = FACE * (f ^ 1)
        stack = jnp.concatenate([trace[v][opposite:opposite + FACE] for v in range(5)], axis=0)
        found = pick(stack, one_hot(local_key, neigh[f:f + 1]))
        outer.append(found)
    nodes = nodes_ref[...]
    nodes = jnp.where(nodes >= owned, nodes + (own_pad - owned), nodes)
    nodes = jnp.concatenate([nodes[k:k + 1] for k in range(8)], axis=1)
    table_rows = lax.broadcasted_iota(jnp.int32, (own_pad + halo_pad, 8 * elements), 0)
    corner_hot = one_hot(table_rows, nodes)

    def corners_of(table):
        found = pick(table, corner_hot)
        return [
            jnp.concatenate(
                [found[i:i + 1, k * elements:(k + 1) * elements] for k in range(8)], axis=0
            )
            for i in range(3)
        ]

    geo = geo_ref[...].astype(BF16)

    def edges_of(corners):
        hi, mid, lo = split(jnp.concatenate(corners, axis=1), 3)
        out = jnp.dot(geo, rows_of([hi, mid, lo, hi, mid, hi]), preferred_element_type=F32)
        rows = [out[:, i * elements:(i + 1) * elements] for i in range(3)]
        volume = [[rows[i][POINTS * j:POINTS * (j + 1)] for i in range(3)] for j in range(3)]
        base = 3 * POINTS
        first = [rows[i][base:base + 6 * FACE] for i in range(3)]
        second = [rows[i][base + 6 * FACE:base + 12 * FACE] for i in range(3)]
        lap = [rows[i][base + 12 * FACE:] for i in range(3)]
        return volume, first, second, lap

    place_copy.wait()
    corners = corners_of(jnp.concatenate([places, place_in[...]], axis=1))
    edge, first, second, lap = edges_of(corners)
    normals = [cross(edge[(j + 1) % 3], edge[(j + 2) % 3]) for j in range(3)]
    face_n = cross(first, second)
    square = dot3(face_n, face_n)
    size = jnp.sqrt(square)

    flux = [gas.along(normals[j]) for j in range(3)]
    inner = Gas([t[:, :elements] for t in trace])
    inner_speed, inner_grad = inner.speed(face_n, square, size)

    up_copy.wait()
    outer[0] = outer[0] + pick(up_in[...], one_hot(halo_key, neigh[0:1]))
    down_copy.wait()
    outer[1] = outer[1] + pick(down_in[...], one_hot(halo_key, neigh[1:2]))
    side = []
    for v in range(5):
        side.append(
            jnp.concatenate(
                [
                    outer[f][FACE * v:FACE * (v + 1)] + far[f:f + 1] * far_field[:, v:v + 1]
                    for f in range(6)
                ],
                axis=0,
            )
        )
    other = Gas([t[:, :elements] for t in side])
    other_speed, other_grad = other.speed(face_n, square, size)
    gap = inner_speed - other_speed
    root = jnp.sqrt(gap * gap + SOFT * square)
    inv_root = 0.5 / root
    lam = 0.5 * (inner_speed + other_speed) + 0.5 * root
    lam_n = [
        0.5 * (inner_grad[i] + other_grad[i])
        + (gap * (inner_grad[i] - other_grad[i]) + SOFT * face_n[i]) * inv_root
        for i in range(3)
    ]
    diff = [other.u[v] - inner.u[v] for v in range(5)]
    inner_along, other_along = inner.along(face_n), other.along(face_n)
    asm = asm_ref[...].astype(BF16)
    columns = []
    for v in range(5):
        jump = 0.5 * (other_along[v] - inner_along[v] - lam * diff[v])
        columns.append(jnp.concatenate([flux[0][v], flux[1][v], flux[2][v], jump], axis=0))
    result = apply_table(asm, jnp.concatenate(columns, axis=1))
    weighted = []
    for v in range(5):
        residual = result[:, v * elements:(v + 1) * elements]
        res_ref[v] = residual
        weighted.append(residual * weight)
    stores[0].start()

    asm_t = asm_t_ref[...].astype(BF16)
    back = [apply_table(asm_t, weighted[v]) for v in range(5)]
    grads = [gas.against([b[POINTS * j:POINTS * (j + 1)] for b in back]) for j in range(3)]
    face_back = [b[3 * POINTS:] for b in back]
    across = sum(face_back[v] * diff[v] for v in range(5))
    inner_against, other_against = inner.against(face_back), other.against(face_back)
    face_grad = [
        0.5 * (other_against[i] - inner_against[i] - across * lam_n[i]) for i in range(3)
    ]
    edge_grad = []
    for j in range(3):
        one = cross(edge[(j + 1) % 3], grads[(j + 2) % 3])
        two = cross(grads[(j + 1) % 3], edge[(j + 2) % 3])
        edge_grad.append([one[i] + two[i] for i in range(3)])
    first_grad, second_grad = cross(second, face_grad), cross(face_grad, first)
    smoothing = damping[:, 1:2]
    geo_t = geo_t_ref[...].astype(BF16)
    stack = [
        jnp.concatenate(
            [edge_grad[0][i], edge_grad[1][i], edge_grad[2][i], first_grad[i], second_grad[i]], axis=0
        )
        for i in range(3)
    ]
    pulled = apply_table(geo_t, jnp.concatenate(stack, axis=1))
    rows = []
    for i in range(3):
        corner_grad = pulled[:, i * elements:(i + 1) * elements] + smoothing * weight * lap[i]
        rows.append(jnp.concatenate([corner_grad[k:k + 1] for k in range(8)], axis=1))
    rows.append(jnp.concatenate([weight] * 8, axis=1))
    rows.append(jnp.zeros((4, 8 * elements), F32))
    table = pick_t(jnp.concatenate(rows, axis=0), corner_hot)
    own_part, halo_part = table[:, :own_pad], table[:, own_pad:]

    gup_out[...] = halo_part
    gup_copy = remote(3, gup_out, gup_in, right)
    gup_copy.start()
    gdown_out[...] = pick(own_part, sent_nodes)
    gdown_copy = remote(4, gdown_out, gdown_in, left)
    gdown_copy.start()

    gas.vary(tangent)
    inner.vary([t[:, elements:] for t in trace])
    other.vary([t[:, elements:] for t in side])
    flux_change = [gas.along_change(normals[j]) for j in range(3)]
    inner_dspeed, other_dspeed = inner.speed_change(face_n, size), other.speed_change(face_n, size)
    dlam = 0.5 * (inner_dspeed + other_dspeed) + gap * (inner_dspeed - other_dspeed) * inv_root
    inner_change, other_change = inner.along_change(face_n), other.along_change(face_n)
    columns = []
    for v in range(5):
        ddiff = other.du[v] - inner.du[v]
        djump = 0.5 * (other_change[v] - inner_change[v] - dlam * diff[v] - lam * ddiff)
        columns.append(
            jnp.concatenate([flux_change[0][v], flux_change[1][v], flux_change[2][v], djump], axis=0)
        )
    result = apply_table(asm, jnp.concatenate(columns, axis=1))
    for v in range(5):
        change_ref[v] = result[:, v * elements:(v + 1) * elements]
    stores[1].start()

    def descent_of(total):
        line = lax.broadcasted_iota(jnp.int32, total.shape, 0)
        touched = jnp.where(total[3:4] > 0.5, 1.0, 0.0)
        return -jnp.where(line < 3, total * touched, 0.0)

    gup_copy.wait()
    descent = descent_of(own_part + pick_t(gup_in[...], sent_nodes))
    gdown_copy.wait()
    halo_descent = descent_of(halo_part + gdown_in[...])

    steps = corners_of(jnp.concatenate([descent, halo_descent], axis=1))
    dedge, dfirst, dsecond, dlap = edges_of(steps)
    dflux = []
    for j in range(3):
        a, b = (j + 1) % 3, (j + 2) % 3
        one, two = cross(dedge[a], edge[b]), cross(edge[a], dedge[b])
        dflux.append(gas.along([one[i] + two[i] for i in range(3)]))
    one, two = cross(dfirst, second), cross(first, dsecond)
    dface = [one[i] + two[i] for i in range(3)]
    inner_dalong, other_dalong = inner.along(dface), other.along(dface)
    dlam_n = dot3(lam_n, dface)
    columns = []
    for v in range(5):
        jump = 0.5 * (other_dalong[v] - inner_dalong[v] - dlam_n * diff[v])
        columns.append(jnp.concatenate([dflux[0][v], dflux[1][v], dflux[2][v], jump], axis=0))
    moved = apply_table(asm, jnp.concatenate(columns, axis=1))
    squares = jnp.sum(moved * moved, axis=0, keepdims=True)
    squares = sum(squares[:, v * elements:(v + 1) * elements] for v in range(5))
    curvature = squares * weight
    bent = sum(steps[i] * dlap[i] for i in range(3))
    bending = smoothing * jnp.sum(bent, axis=0, keepdims=True) * weight
    norm = jnp.sum(descent * descent, axis=0, keepdims=True)
    both_sums = jnp.sum(curvature + bending, axis=1, keepdims=True)
    norm_sum = jnp.sum(norm, axis=1, keepdims=True)
    line = lax.broadcasted_iota(jnp.int32, (8, LANES), 0)
    sums = jnp.where(line == 0, norm_sum, jnp.where(line == 1, both_sums, 0.0))

    index = 0
    for s, stage in enumerate(stages):
        sum_out[s] = sums
        copies = []
        for _ in stage:
            copies.append(remote(5 + index, sum_out.at[s], sum_in.at[index], partners[index]))
            copies[-1].start()
            index += 1
        for i, copy in enumerate(copies):
            copy.wait_recv()
        for i in range(len(stage)):
            sums = sums + sum_in[index - len(stage) + i]
        for copy in copies:
            copy.wait_send()
    norm_total, rest = sums[0:1, 0:1], sums[1:2, 0:1]
    step_size = norm_total / (rest + damping[:, 0:1] * norm_total)
    update_ref[...] = (descent * step_size)[0:3, :owned]
    stores[2].start()
    for store in stores:
        store.wait()


def write_out(*refs):
    loads = [pltpu.make_async_copy(refs[i], refs[6 + i], refs[9].at[i]) for i in range(3)]
    stores = [pltpu.make_async_copy(refs[6 + i], refs[3 + i], refs[9].at[3 + i]) for i in range(3)]
    for load in loads:
        load.start()
    for load, store in zip(loads, stores):
        load.wait()
        store.start()
    for store in stores:
        store.wait()


def body(n, group, flow_state, state_tangent, far_field, coordinates, damping, face_neighbour,
         element_nodes, upper_sends, lower_sends, node_sends, shock_flags):
    own_pad = -(-coordinates.shape[1] // LANES) * LANES
    halo_pad = -(-node_sends.shape[0] // LANES) * LANES
    wide = 2 * flow_state.shape[2]
    count, stages, low = 0, 0, 1
    while low < n:
        size = min(group, n // low)
        count, stages, low = count + size - 1, stages + 1, low * size
    hbm = pl.BlockSpec(memory_space=pltpu.HBM)
    constants = [jnp.asarray(t) for t in tables()]
    halo = pltpu.VMEM((5 * FACE, wide), F32)
    place = pltpu.VMEM((8, halo_pad), F32)
    operands = [
        flow_state, state_tangent, far_field.reshape(1, -1), coordinates, damping.reshape(1, -1),
        face_neighbour, element_nodes,
        upper_sends.reshape(1, -1), lower_sends.reshape(1, -1), node_sends.reshape(1, -1),
        shock_flags.reshape(1, -1),
    ] + constants
    shapes = (
        jax.ShapeDtypeStruct(flow_state.shape, F32),
        jax.ShapeDtypeStruct(flow_state.shape, F32),
        jax.ShapeDtypeStruct(coordinates.shape, F32),
    )
    results = pl.pallas_call(
        functools.partial(kernel, n, group),
        out_shape=shapes,
        in_specs=[hbm] * len(operands),
        out_specs=(hbm, hbm, hbm),
        scratch_shapes=[pltpu.VMEM(o.shape, o.dtype) for o in operands + list(shapes)] + [halo] * 4 + [place] * 6 + [
            pltpu.VMEM((stages, 8, LANES), F32),
            pltpu.VMEM((count, 8, LANES), F32),
            pltpu.SemaphoreType.DMA((5 + count,)),
            pltpu.SemaphoreType.DMA((5 + count,)),
            pltpu.SemaphoreType.DMA((INPUTS + 3,)),
        ],
        compiler_params=pltpu.CompilerParams(
            collective_id=0, has_side_effects=True, vmem_limit_bytes=VMEM_LIMIT
        ),
    )(*operands)
    return pl.pallas_call(
        write_out,
        out_shape=shapes,
        in_specs=[hbm] * 3,
        out_specs=[hbm] * 3,
        scratch_shapes=[pltpu.VMEM(o.shape, o.dtype) for o in shapes] + [pltpu.SemaphoreType.DMA((6,))],
        compiler_params=pltpu.CompilerParams(vmem_limit_bytes=VMEM_LIMIT),
    )(*results)


def solution(mesh):
    n = mesh.shape["parts"]
    in_specs = (
        P(None, None, "parts"),
        P(None, None, "parts"),
        P(),
        P(None, "parts"),
        P(),
        P(None, "parts"),
        P(None, "parts"),
        P("parts"),
        P("parts"),
        P("parts"),
        P("parts"),
    )
    out_specs = (P(None, None, "parts"), P(None, None, "parts"), P(None, "parts"))
    return jax.shard_map(
        functools.partial(body, n, 8), mesh=mesh, in_specs=in_specs, out_specs=out_specs,
        check_vma=False,
    )
```

profile of v0, /device:TPU:0, one launch (start us, length us, event | category | flops | bytes accessed | tf_op | source)
XLA Modules:
  0.0 27.0 jit_solution(18400160041723296006)
XLA Ops:
  0.6 24.6 %shard_map.175 = (f32[5,64,64]{2,1,0:T(8,128)}, f32[5,64,64]{2,1,0:T(8,128)}, f32[3,102]{1,0:T(4,128)}) custom-call(f32[5,64,64]{2,1,0:T(8,128)} %refs_0_.1, f32[5,64,64]{2,1,0:T(8,128)} %refs_1_.1, f32[1,5]{1,0:T(1,128)} %bitcast.6, f32[3,102]{1,0:T(4,128)} %refs_3_.1, f32[1,2]{1,0:T(1,128)} %bitcast.7, s32[6,64]{1,0:T(8,128)} %refs_5_.1, s32[8,64]{1,0:T(8,128)} %refs_6_.1, ...), custom_call_target="tpu_custom_call" | custom-call | tf_op jit(solution)/shard_map/pallas_call | solution.py:569
  25.3 1.7 %shard_map.176 = (f32[5,64,64]{2,1,0:T(8,128)}, f32[5,64,64]{2,1,0:T(8,128)}, f32[3,102]{1,0:T(4,128)}) custom-call(f32[5,64,64]{2,1,0:T(8,128)} %get-tuple-element.6.refs_0_, f32[5,64,64]{2,1,0:T(8,128)} %get-tuple-element.7.refs_1_, f32[3,102]{1,0:T(4,128)} %get-tuple-element.8.refs_2_), custom_call_target="tpu_custom_call" | custom-call | tf_op jit(solution)/shard_map/pallas_call | solution.py:585
where the time goes:
time: 27.1 us; the launch traced here: 27 us
  Pallas kernels  26.3 us (97%)
  between operations  0.64 us (2%)
    pallas_call x1, Pallas kernels, body(): pl.pallas_call(functools.partial(kernel, n, group), out_shape=shapes, in_...  24.6 us
    pallas_call x1, Pallas kernels, body(): pl.pallas_call(write_out, out_shape=shapes, in_specs=[hbm] * 3, out_specs...  1.71 us

commit v1 on v0

--- a/solution.py
+++ b/solution.py
@@ -15,12 +15,14 @@
 F32 = jnp.float32
 BF16 = jnp.bfloat16
 OTHER = 4096
+FACE = 16
+POINTS = 64
 INPUTS = 16
+ROWS = 8
+GEO = 12 * FACE + 3 * POINTS + 8
 VMEM_LIMIT = 60 * 1024 * 1024
 LOAD_ORDER = (9, 3, 7, 8, 0, 1, 11, 5, 6, 14, 2, 4, 10, 12, 13, 15)
 LANES = 128
-FACE = 16
-POINTS = 64
 
 
 def lobatto_tables():
@@ -162,12 +164,18 @@
 
 
 class Gas:
-    def __init__(self, values):
+    def __init__(self, values, saved=None):
         self.u, self.m = values, values[1:4]
+        if saved is not None:
+            self.inv, self.p, self.h, *self.v = saved
+            return
         self.inv = 1.0 / values[0]
         self.v = [m * self.inv for m in self.m]
         self.p = 0.4 * (values[4] - 0.5 * dot3(self.m, self.v))
         self.h = values[4] + self.p
+
+    def saved(self):
+        return [self.inv, self.p, self.h] + self.v
 
     def vary(self, tangent):
         self.du, self.dm = tangent, tangent[1:4]
@@ -202,6 +210,14 @@
         return self.slope * dot3(self.dv, n) + dsound * size
 
 
+def chunks(count, step):
+    def one(c, carry):
+        step(pl.multiple_of(c * ROWS, ROWS))
+        return carry
+
+    lax.fori_loop(0, count // ROWS, one, 0, unroll=2)
+
+
 def kernel(n, group, *refs):
     sources, refs = refs[:INPUTS], refs[INPUTS:]
     results, refs = refs[:3], refs[3:]
@@ -210,7 +226,8 @@
     (state_ref, tangent_ref, far_ref, place_ref, damp_ref, neigh_ref, nodes_ref, upper_ref, lower_ref,
      sends_ref, flag_ref, select_ref, asm_ref, asm_t_ref, geo_ref, geo_t_ref) = held
     (up_out, up_in, down_out, down_in, place_out, place_in,
-     gup_out, gup_in, gdown_out, gdown_in, sum_out, sum_in, send_sem, recv_sem, load_sem) = refs
+     gup_out, gup_in, gdown_out, gdown_in, sum_out, sum_in, send_sem, recv_sem, load_sem,
+     trace_s, side_s, geo_s, dgeo_s, vol_s, face_s, x_s, back_s, pull_s) = refs
     loads = [
         pltpu.make_async_copy(sources[i], held[i], load_sem.at[i]) for i in range(INPUTS)
     ]
@@ -316,11 +333,11 @@
     weight = flag_ref[...].astype(F32)
     far_field = far_ref[...]
     damping = damp_ref[...]
-    gas = Gas(values)
     select = select_ref[...].astype(BF16)
     traces = jnp.dot(
         select, rows_of(split(jnp.concatenate(both, axis=1), 3)), preferred_element_type=F32
     )
+    trace_s[...] = traces
     trace = [traces[:, v * wide:(v + 1) * wide] for v in range(5)]
     neigh = neigh_ref[...]
     neigh = jnp.concatenate([neigh, neigh + OTHER], axis=1)
@@ -348,63 +365,100 @@
 
     geo = geo_ref[...].astype(BF16)
 
-    def edges_of(corners):
-        hi, mid, lo = split(jnp.concatenate(corners, axis=1), 3)
-        out = jnp.dot(geo, rows_of([hi, mid, lo, hi, mid, hi]), preferred_element_type=F32)
-        rows = [out[:, i * elements:(i + 1) * elements] for i in range(3)]
-        volume = [[rows[i][POINTS * j:POINTS * (j + 1)] for i in range(3)] for j in range(3)]
-        base = 3 * POINTS
-        first = [rows[i][base:base + 6 * FACE] for i in range(3)]
-        second = [rows[i][base + 6 * FACE:base + 12 * FACE] for i in range(3)]
-        lap = [rows[i][base + 12 * FACE:] for i in range(3)]
-        return volume, first, second, lap
+    def edges_of(corners, out):
+        for i in range(3):
+            hi, mid, lo = split(corners[i], 3)
+            out[i] = jnp.dot(geo, rows_of([hi, mid, lo, hi, mid, hi]), preferred_element_type=F32)
+
+    base = 3 * POINTS
+    sides = 6 * FACE
+
+    def volume_edges(source, r):
+        return [[source[i, pl.ds(POINTS * j + r, ROWS)] for i in range(3)] for j in range(3)]
+
+    def face_edges(source, r):
+        first = [source[i, pl.ds(base + r, ROWS)] for i in range(3)]
+        second = [source[i, pl.ds(base + sides + r, ROWS)] for i in range(3)]
+        return first, second
+
+    def put(target, r, values, at=0):
+        for k, value in enumerate(values):
+            target[at + k, pl.ds(r, ROWS)] = value
+
+    def take(source, r, count, at=0):
+        return [source[at + k, pl.ds(r, ROWS)] for k in range(count)]
+
+    def lanes(source, r, tangent_half):
+        at = elements if tangent_half else 0
+        return [source[pl.ds(r, ROWS), v * wide + at:v * wide + at + elements] for v in range(5)]
+
+    def volume_gas(r):
+        return Gas(take(state_ref, r, 5), take(vol_s, r, 6))
+
+    def face_gas(r):
+        inner = Gas(lanes(trace_s, r, False), take(face_s, r, 6))
+        other = Gas(lanes(side_s, r, False), take(face_s, r, 6, 6))
+        return inner, other
 
     place_copy.wait()
     corners = corners_of(jnp.concatenate([places, place_in[...]], axis=1))
-    edge, first, second, lap = edges_of(corners)
-    normals = [cross(edge[(j + 1) % 3], edge[(j + 2) % 3]) for j in range(3)]
-    face_n = cross(first, second)
-    square = dot3(face_n, face_n)
-    size = jnp.sqrt(square)
-
-    flux = [gas.along(normals[j]) for j in range(3)]
-    inner = Gas([t[:, :elements] for t in trace])
-    inner_speed, inner_grad = inner.speed(face_n, square, size)
+    edges_of(corners, geo_s)
+    lap = [geo_s[i, base + 2 * sides:] for i in range(3)]
+
+    def volume_flux(r):
+        edge = volume_edges(geo_s, r)
+        gas = Gas(take(state_ref, r, 5))
+        put(vol_s, r, gas.saved())
+        for j in range(3):
+            normal = cross(edge[(j + 1) % 3], edge[(j + 2) % 3])
+            put(vol_s, r, normal, 6 + 3 * j)
+            put(x_s, POINTS * j + r, gas.along(normal))
+
+    chunks(POINTS, volume_flux)
 
     up_copy.wait()
     outer[0] = outer[0] + pick(up_in[...], one_hot(halo_key, neigh[0:1]))
     down_copy.wait()
     outer[1] = outer[1] + pick(down_in[...], one_hot(halo_key, neigh[1:2]))
-    side = []
     for v in range(5):
-        side.append(
-            jnp.concatenate(
-                [
-                    outer[f][FACE * v:FACE * (v + 1)] + far[f:f + 1] * far_field[:, v:v + 1]
-                    for f in range(6)
-                ],
-                axis=0,
-            )
+        side_s[:, v * wide:(v + 1) * wide] = jnp.concatenate(
+            [
+                outer[f][FACE * v:FACE * (v + 1)] + far[f:f + 1] * far_field[:, v:v + 1]
+                for f in range(6)
+            ],
+            axis=0,
         )
-    other = Gas([t[:, :elements] for t in side])
-    other_speed, other_grad = other.speed(face_n, square, size)
-    gap = inner_speed - other_speed
-    root = jnp.sqrt(gap * gap + SOFT * square)
-    inv_root = 0.5 / root
-    lam = 0.5 * (inner_speed + other_speed) + 0.5 * root
-    lam_n = [
-        0.5 * (inner_grad[i] + other_grad[i])
-        + (gap * (inner_grad[i] - other_grad[i]) + SOFT * face_n[i]) * inv_root
-        for i in range(3)
-    ]
-    diff = [other.u[v] - inner.u[v] for v in range(5)]
-    inner_along, other_along = inner.along(face_n), other.along(face_n)
+
+    def face_flux(r):
+        face_n = cross(*face_edges(geo_s, r))
+        square = dot3(face_n, face_n)
+        size = jnp.sqrt(square)
+        inner, other = Gas(lanes(trace_s, r, False)), Gas(lanes(side_s, r, False))
+        inner_speed, inner_grad = inner.speed(face_n, square, size)
+        other_speed, other_grad = other.speed(face_n, square, size)
+        gap = inner_speed - other_speed
+        root = jnp.sqrt(gap * gap + SOFT * square)
+        inv_root = 0.5 / root
+        lam = 0.5 * (inner_speed + other_speed) + 0.5 * root
+        lam_n = [
+            0.5 * (inner_grad[i] + other_grad[i])
+            + (gap * (inner_grad[i] - other_grad[i]) + SOFT * face_n[i]) * inv_root
+            for i in range(3)
+        ]
+        one, two = inner.along(face_n), other.along(face_n)
+        jump = [0.5 * (two[v] - one[v] - lam * (other.u[v] - inner.u[v])) for v in range(5)]
+        put(x_s, base + r, jump)
+        put(face_s, r, inner.saved() + other.saved() + face_n + lam_n)
+        rest = [size, lam, gap * inv_root, inner.slope, inner.sound, other.slope, other.sound]
+        put(face_s, r, rest, 18)
+
+    chunks(sides, face_flux)
     asm = asm_ref[...].astype(BF16)
-    columns = []
-    for v in range(5):
-        jump = 0.5 * (other_along[v] - inner_along[v] - lam * diff[v])
-        columns.append(jnp.concatenate([flux[0][v], flux[1][v], flux[2][v], jump], axis=0))
-    result = apply_table(asm, jnp.concatenate(columns, axis=1))
+
+    def assembled():
+        return apply_table(asm, jnp.concatenate([x_s[v] for v in range(5)], axis=1))
+
+    result = assembled()
     weighted = []
     for v in range(5):
         residual = result[:, v * elements:(v + 1) * elements]
@@ -413,29 +467,34 @@
     stores[0].start()
 
     asm_t = asm_t_ref[...].astype(BF16)
-    back = [apply_table(asm_t, weighted[v]) for v in range(5)]
-    grads = [gas.against([b[POINTS * j:POINTS * (j + 1)] for b in back]) for j in range(3)]
-    face_back = [b[3 * POINTS:] for b in back]
-    across = sum(face_back[v] * diff[v] for v in range(5))
-    inner_against, other_against = inner.against(face_back), other.against(face_back)
-    face_grad = [
-        0.5 * (other_against[i] - inner_against[i] - across * lam_n[i]) for i in range(3)
-    ]
-    edge_grad = []
-    for j in range(3):
-        one = cross(edge[(j + 1) % 3], grads[(j + 2) % 3])
-        two = cross(grads[(j + 1) % 3], edge[(j + 2) % 3])
-        edge_grad.append([one[i] + two[i] for i in range(3)])
-    first_grad, second_grad = cross(second, face_grad), cross(face_grad, first)
+    for v in range(5):
+        back_s[v] = apply_table(asm_t, weighted[v])
+
+    def volume_pull(r):
+        edge = volume_edges(geo_s, r)
+        gas = volume_gas(r)
+        grads = [gas.against(take(back_s, POINTS * j + r, 5)) for j in range(3)]
+        for j in range(3):
+            one = cross(edge[(j + 1) % 3], grads[(j + 2) % 3])
+            two = cross(grads[(j + 1) % 3], edge[(j + 2) % 3])
+            put(pull_s, POINTS * j + r, [one[i] + two[i] for i in range(3)])
+
+    def face_pull(r):
+        first, second = face_edges(geo_s, r)
+        inner, other = face_gas(r)
+        lam_n = take(face_s, r, 3, 15)
+        y = take(back_s, base + r, 5)
+        across = sum(y[v] * (other.u[v] - inner.u[v]) for v in range(5))
+        one, two = inner.against(y), other.against(y)
+        grad = [0.5 * (two[i] - one[i] - across * lam_n[i]) for i in range(3)]
+        put(pull_s, base + r, cross(second, grad))
+        put(pull_s, base + sides + r, cross(grad, first))
+
+    chunks(POINTS, volume_pull)
+    chunks(sides, face_pull)
     smoothing = damping[:, 1:2]
     geo_t = geo_t_ref[...].astype(BF16)
-    stack = [
-        jnp.concatenate(
-            [edge_grad[0][i], edge_grad[1][i], edge_grad[2][i], first_grad[i], second_grad[i]], axis=0
-        )
-        for i in range(3)
-    ]
-    pulled = apply_table(geo_t, jnp.concatenate(stack, axis=1))
+    pulled = apply_table(geo_t, jnp.concatenate([pull_s[i] for i in range(3)], axis=1))
     rows = []
     for i in range(3):
         corner_grad = pulled[:, i * elements:(i + 1) * elements] + smoothing * weight * lap[i]
@@ -452,21 +511,30 @@
     gdown_copy = remote(4, gdown_out, gdown_in, left)
     gdown_copy.start()
 
-    gas.vary(tangent)
-    inner.vary([t[:, elements:] for t in trace])
-    other.vary([t[:, elements:] for t in side])
-    flux_change = [gas.along_change(normals[j]) for j in range(3)]
-    inner_dspeed, other_dspeed = inner.speed_change(face_n, size), other.speed_change(face_n, size)
-    dlam = 0.5 * (inner_dspeed + other_dspeed) + gap * (inner_dspeed - other_dspeed) * inv_root
-    inner_change, other_change = inner.along_change(face_n), other.along_change(face_n)
-    columns = []
-    for v in range(5):
-        ddiff = other.du[v] - inner.du[v]
-        djump = 0.5 * (other_change[v] - inner_change[v] - dlam * diff[v] - lam * ddiff)
-        columns.append(
-            jnp.concatenate([flux_change[0][v], flux_change[1][v], flux_change[2][v], djump], axis=0)
-        )
-    result = apply_table(asm, jnp.concatenate(columns, axis=1))
+    def volume_change(r):
+        gas = volume_gas(r)
+        gas.vary(take(tangent_ref, r, 5))
+        for j in range(3):
+            put(x_s, POINTS * j + r, gas.along_change(take(vol_s, r, 3, 6 + 3 * j)))
+
+    def face_change(r):
+        inner, other = face_gas(r)
+        inner.vary(lanes(trace_s, r, True))
+        other.vary(lanes(side_s, r, True))
+        face_n = take(face_s, r, 3, 12)
+        size, lam, lean, inner.slope, inner.sound, other.slope, other.sound = take(face_s, r, 7, 18)
+        ds, dt = inner.speed_change(face_n, size), other.speed_change(face_n, size)
+        dlam = 0.5 * (ds + dt) + lean * (ds - dt)
+        one, two = inner.along_change(face_n), other.along_change(face_n)
+        jump = []
+        for v in range(5):
+            moved = dlam * (other.u[v] - inner.u[v]) + lam * (other.du[v] - inner.du[v])
+            jump.append(0.5 * (two[v] - one[v] - moved))
+        put(x_s, base + r, jump)
+
+    chunks(POINTS, volume_change)
+    chunks(sides, face_change)
+    result = assembled()
     for v in range(5):
         change_ref[v] = result[:, v * elements:(v + 1) * elements]
     stores[1].start()
@@ -482,21 +550,31 @@
     halo_descent = descent_of(halo_part + gdown_in[...])
 
     steps = corners_of(jnp.concatenate([descent, halo_descent], axis=1))
-    dedge, dfirst, dsecond, dlap = edges_of(steps)
-    dflux = []
-    for j in range(3):
-        a, b = (j + 1) % 3, (j + 2) % 3
-        one, two = cross(dedge[a], edge[b]), cross(edge[a], dedge[b])
-        dflux.append(gas.along([one[i] + two[i] for i in range(3)]))
-    one, two = cross(dfirst, second), cross(first, dsecond)
-    dface = [one[i] + two[i] for i in range(3)]
-    inner_dalong, other_dalong = inner.along(dface), other.along(dface)
-    dlam_n = dot3(lam_n, dface)
-    columns = []
-    for v in range(5):
-        jump = 0.5 * (other_dalong[v] - inner_dalong[v] - dlam_n * diff[v])
-        columns.append(jnp.concatenate([dflux[0][v], dflux[1][v], dflux[2][v], jump], axis=0))
-    moved = apply_table(asm, jnp.concatenate(columns, axis=1))
+    edges_of(steps, dgeo_s)
+    dlap = [dgeo_s[i, base + 2 * sides:] for i in range(3)]
+
+    def volume_step(r):
+        edge, dedge = volume_edges(geo_s, r), volume_edges(dgeo_s, r)
+        gas = volume_gas(r)
+        for j in range(3):
+            a, b = (j + 1) % 3, (j + 2) % 3
+            one, two = cross(dedge[a], edge[b]), cross(edge[a], dedge[b])
+            put(x_s, POINTS * j + r, gas.along([one[i] + two[i] for i in range(3)]))
+
+    def face_step(r):
+        first, second = face_edges(geo_s, r)
+        dfirst, dsecond = face_edges(dgeo_s, r)
+        inner, other = face_gas(r)
+        one, two = cross(dfirst, second), cross(first, dsecond)
+        dface = [one[i] + two[i] for i in range(3)]
+        dlam = dot3(take(face_s, r, 3, 15), dface)
+        one, two = inner.along(dface), other.along(dface)
+        jump = [0.5 * (two[v] - one[v] - dlam * (other.u[v] - inner.u[v])) for v in range(5)]
+        put(x_s, base + r, jump)
+
+    chunks(POINTS, volume_step)
+    chunks(sides, face_step)
+    moved = assembled()
     squares = jnp.sum(moved * moved, axis=0, keepdims=True)
     squares = sum(squares[:, v * elements:(v + 1) * elements] for v in range(5))
     curvature = squares * weight
@@ -577,6 +655,15 @@
             pltpu.SemaphoreType.DMA((5 + count,)),
             pltpu.SemaphoreType.DMA((5 + count,)),
             pltpu.SemaphoreType.DMA((INPUTS + 3,)),
+            pltpu.VMEM((6 * FACE, 5 * wide), F32),
+            pltpu.VMEM((6 * FACE, 5 * wide), F32),
+            pltpu.VMEM((3, GEO, wide // 2), F32),
+            pltpu.VMEM((3, GEO, wide // 2), F32),
+            pltpu.VMEM((15, POINTS, wide // 2), F32),
+            pltpu.VMEM((25, 6 * FACE, wide // 2), F32),
+            pltpu.VMEM((5, 3 * POINTS + 6 * FACE, wide // 2), F32),
+            pltpu.VMEM((5, 3 * POINTS + 6 * FACE, wide // 2), F32),
+            pltpu.VMEM((3, 3 * POINTS + 12 * FACE, wide // 2), F32),
         ],
         compiler_params=pltpu.CompilerParams(
             collective_id=0, has_side_effects=True, vmem_limit_bytes=VMEM_LIMIT

time: 27.1 us -> 29.2 us (1.077)
  Pallas kernels: 26.3 us -> 28.4 us
    pallas_call x1, Pallas kernels: 24.6 us -> 26.6 us  [body(): pl.pallas_call(functools.partial(kernel, n, group), out_shape=shapes, in_...]
where the time goes in v1:
time: 29.2 us; the launch traced here: 29 us
  Pallas kernels  28.4 us (97%)
  between operations  0.64 us (2%)
    pallas_call x1, Pallas kernels, body(): pl.pallas_call(functools.partial(kernel, n, group), out_shape=shapes, in_...  26.6 us
    pallas_call x1, Pallas kernels, body(): pl.pallas_call(write_out, out_shape=shapes, in_specs=[hbm] * 3, out_specs...  1.71 us

profile of v1, /device:TPU:0, one launch (start us, length us, event | category | flops | bytes accessed | tf_op | source)
XLA Modules:
  0.0 29.0 jit_solution(9238345566752224035)
XLA Ops:
  0.6 26.6 %shard_map.175 = (f32[5,64,64]{2,1,0:T(8,128)}, f32[5,64,64]{2,1,0:T(8,128)}, f32[3,102]{1,0:T(4,128)}) custom-call(f32[5,64,64]{2,1,0:T(8,128)} %refs_0_.1, f32[5,64,64]{2,1,0:T(8,128)} %refs_1_.1, f32[1,5]{1,0:T(1,128)} %bitcast.6, f32[3,102]{1,0:T(4,128)} %refs_3_.1, f32[1,2]{1,0:T(1,128)} %bitcast.7, s32[6,64]{1,0:T(8,128)} %refs_5_.1, s32[8,64]{1,0:T(8,128)} %refs_6_.1, ...), custom_call_target="tpu_custom_call" | custom-call | tf_op jit(solution)/shard_map/pallas_call | solution.py:647
  27.3 1.7 %shard_map.176 = (f32[5,64,64]{2,1,0:T(8,128)}, f32[5,64,64]{2,1,0:T(8,128)}, f32[3,102]{1,0:T(4,128)}) custom-call(f32[5,64,64]{2,1,0:T(8,128)} %get-tuple-element.6.refs_0_, f32[5,64,64]{2,1,0:T(8,128)} %get-tuple-element.7.refs_1_, f32[3,102]{1,0:T(4,128)} %get-tuple-element.8.refs_2_), custom_call_target="tpu_custom_call" | custom-call | tf_op jit(solution)/shard_map/pallas_call | solution.py:672

commit v2 on v0

--- a/solution.py
+++ b/solution.py
@@ -15,9 +15,9 @@
 F32 = jnp.float32
 BF16 = jnp.bfloat16
 OTHER = 4096
-INPUTS = 16
+INPUTS = 17
 VMEM_LIMIT = 60 * 1024 * 1024
-LOAD_ORDER = (9, 3, 7, 8, 0, 1, 11, 5, 6, 14, 2, 4, 10, 12, 13, 15)
+LOAD_ORDER = (9, 3, 7, 8, 0, 1, 11, 5, 6, 15, 2, 4, 10, 12, 13, 14, 16)
 LANES = 128
 FACE = 16
 POINTS = 64
@@ -94,8 +94,9 @@
     tangents = np.concatenate([gradients.reshape(192, 8)] + first + second, axis=0)
     hi, mid, lo = split_table(np.concatenate([tangents, edge_laplacian()], axis=0))
     arrays = (
-        np.concatenate([select] * 3, axis=1),
-        two_parts(assembly),
+        np.concatenate([select] * 2, axis=1),
+        two_parts(np.concatenate([assembly[:, :192], assembly[:, 224:]], axis=1)),
+        two_parts(assembly[:, 192:224]),
         two_parts(assembly.T),
         np.concatenate([hi, hi, hi, mid, mid, lo], axis=1),
         two_parts(tangents.T),
@@ -135,10 +136,10 @@
     return jnp.dot(table, rows_of([hi, hi, lo]), preferred_element_type=F32)
 
 
-def pick(data, hot):
+def pick(data, hot, parts=3):
     count = data.shape[0]
-    out = jnp.dot(rows_of(split(data, 3)), hot, preferred_element_type=F32)
-    return out[:count] + out[count:2 * count] + out[2 * count:]
+    out = jnp.dot(rows_of(split(data, parts)), hot, preferred_element_type=F32)
+    return sum(out[k * count:(k + 1) * count] for k in range(parts))
 
 
 def pick_t(data, hot):
@@ -159,6 +160,12 @@
 
 def dot3(a, b):
     return a[0] * b[0] + a[1] * b[1] + a[2] * b[2]
+
+
+def stacked(a, b):
+    if isinstance(a, list):
+        return [stacked(x, y) for x, y in zip(a, b)]
+    return jnp.concatenate([a, b], axis=0)
 
 
 class Gas:
@@ -174,6 +181,13 @@
         self.dv = [(self.dm[i] - self.v[i] * tangent[0]) * self.inv for i in range(3)]
         self.dp = 0.4 * (tangent[4] - 0.5 * (dot3(self.dm, self.v) + dot3(self.m, self.dv)))
         self.dh = tangent[4] + self.dp
+
+    @staticmethod
+    def merged(a, b):
+        both = Gas.__new__(Gas)
+        for name, low in vars(a).items():
+            setattr(both, name, stacked(low, getattr(b, name)))
+        return both
 
     def along(self, n):
         vn = dot3(self.v, n)
@@ -208,7 +222,7 @@
     held, refs = refs[:INPUTS], refs[INPUTS:]
     (res_ref, change_ref, update_ref), refs = refs[:3], refs[3:]
     (state_ref, tangent_ref, far_ref, place_ref, damp_ref, neigh_ref, nodes_ref, upper_ref, lower_ref,
-     sends_ref, flag_ref, select_ref, asm_ref, asm_t_ref, geo_ref, geo_t_ref) = held
+     sends_ref, flag_ref, select_ref, asm_ref, asm_halo_ref, asm_t_ref, geo_ref, geo_t_ref) = held
     (up_out, up_in, down_out, down_in, place_out, place_in,
      gup_out, gup_in, gdown_out, gdown_in, sum_out, sum_in, send_sem, recv_sem, load_sem) = refs
     loads = [
@@ -298,10 +312,10 @@
     both = [jnp.concatenate([values[v], tangent[v]], axis=1) for v in range(5)]
     top = POINTS - FACE
     up_out[...] = pick(
-        jnp.concatenate([both[v][top:POINTS] for v in range(5)], axis=0), send_hot(upper_ref[...])
+        jnp.concatenate([both[v][top:POINTS] for v in range(5)], axis=0), send_hot(upper_ref[...]), 2
     )
     down_out[...] = pick(
-        jnp.concatenate([both[v][0:FACE] for v in range(5)], axis=0), send_hot(lower_ref[...])
+        jnp.concatenate([both[v][0:FACE] for v in range(5)], axis=0), send_hot(lower_ref[...]), 2
     )
     pl.semaphore_wait(barrier, 2 + len(partners))
     place_copy = remote(0, place_out, place_in, left)
@@ -319,7 +333,7 @@
     gas = Gas(values)
     select = select_ref[...].astype(BF16)
     traces = jnp.dot(
-        select, rows_of(split(jnp.concatenate(both, axis=1), 3)), preferred_element_type=F32
+        select, rows_of(split(jnp.concatenate(both, axis=1), 2)), preferred_element_type=F32
     )
     trace = [traces[:, v * wide:(v + 1) * wide] for v in range(5)]
     neigh = neigh_ref[...]
@@ -329,7 +343,7 @@
     for f in range(6):
         opposite = FACE * (f ^ 1)
         stack = jnp.concatenate([trace[v][opposite:opposite + FACE] for v in range(5)], axis=0)
-        found = pick(stack, one_hot(local_key, neigh[f:f + 1]))
+        found = pick(stack, one_hot(local_key, neigh[f:f + 1]), 2)
         outer.append(found)
     nodes = nodes_ref[...]
     nodes = jnp.where(nodes >= owned, nodes + (own_pad - owned), nodes)
@@ -359,6 +373,11 @@
         lap = [rows[i][base + 12 * FACE:] for i in range(3)]
         return volume, first, second, lap
 
+    asm = asm_ref[...].astype(BF16)
+    asm_halo = asm_halo_ref[...].astype(BF16)
+    asm_t = asm_t_ref[...].astype(BF16)
+    geo_t = geo_t_ref[...].astype(BF16)
+
     place_copy.wait()
     corners = corners_of(jnp.concatenate([places, place_in[...]], axis=1))
     edge, first, second, lap = edges_of(corners)
@@ -368,43 +387,65 @@
     size = jnp.sqrt(square)
 
     flux = [gas.along(normals[j]) for j in range(3)]
-    inner = Gas([t[:, :elements] for t in trace])
-    inner_speed, inner_grad = inner.speed(face_n, square, size)
-
-    up_copy.wait()
-    outer[0] = outer[0] + pick(up_in[...], one_hot(halo_key, neigh[0:1]))
-    down_copy.wait()
-    outer[1] = outer[1] + pick(down_in[...], one_hot(halo_key, neigh[1:2]))
-    side = []
-    for v in range(5):
-        side.append(
+    split_row = 2 * FACE
+
+    def faces(begin, end):
+        rows = slice(FACE * begin, FACE * end)
+        side = [
             jnp.concatenate(
                 [
                     outer[f][FACE * v:FACE * (v + 1)] + far[f:f + 1] * far_field[:, v:v + 1]
-                    for f in range(6)
+                    for f in range(begin, end)
                 ],
                 axis=0,
             )
-        )
-    other = Gas([t[:, :elements] for t in side])
-    other_speed, other_grad = other.speed(face_n, square, size)
-    gap = inner_speed - other_speed
-    root = jnp.sqrt(gap * gap + SOFT * square)
-    inv_root = 0.5 / root
-    lam = 0.5 * (inner_speed + other_speed) + 0.5 * root
-    lam_n = [
-        0.5 * (inner_grad[i] + other_grad[i])
-        + (gap * (inner_grad[i] - other_grad[i]) + SOFT * face_n[i]) * inv_root
-        for i in range(3)
-    ]
-    diff = [other.u[v] - inner.u[v] for v in range(5)]
-    inner_along, other_along = inner.along(face_n), other.along(face_n)
-    asm = asm_ref[...].astype(BF16)
-    columns = []
-    for v in range(5):
-        jump = 0.5 * (other_along[v] - inner_along[v] - lam * diff[v])
-        columns.append(jnp.concatenate([flux[0][v], flux[1][v], flux[2][v], jump], axis=0))
-    result = apply_table(asm, jnp.concatenate(columns, axis=1))
+            for v in range(5)
+        ]
+        normal, area, extent = [x[rows] for x in face_n], square[rows], size[rows]
+        inner = Gas([t[rows, :elements] for t in trace])
+        other = Gas([t[:, :elements] for t in side])
+        inner_speed, inner_grad = inner.speed(normal, area, extent)
+        other_speed, other_grad = other.speed(normal, area, extent)
+        gap = inner_speed - other_speed
+        root = jnp.sqrt(gap * gap + SOFT * area)
+        inv_root = 0.5 / root
+        lam = 0.5 * (inner_speed + other_speed) + 0.5 * root
+        lam_n = [
+            0.5 * (inner_grad[i] + other_grad[i])
+            + (gap * (inner_grad[i] - other_grad[i]) + SOFT * normal[i]) * inv_root
+            for i in range(3)
+        ]
+        diff = [other.u[v] - inner.u[v] for v in range(5)]
+        one, two = inner.along(normal), other.along(normal)
+        jump = [0.5 * (two[v] - one[v] - lam * diff[v]) for v in range(5)]
+        return inner, other, jump, [side, gap, inv_root, lam, lam_n, diff]
+
+    def local_part(fluxes, jump):
+        data = [
+            jnp.concatenate([fluxes[0][v], fluxes[1][v], fluxes[2][v], jump[v]], axis=0)
+            for v in range(5)
+        ]
+        return apply_table(asm, jnp.concatenate(data, axis=1))
+
+    def halo_part_of(jump):
+        return apply_table(asm_halo, jnp.concatenate(jump, axis=1))
+
+    def assembled(fluxes, jump):
+        first_rows = [x[:split_row] for x in jump]
+        return local_part(fluxes, [x[split_row:] for x in jump]) + halo_part_of(first_rows)
+
+    inner_b, other_b, jump, fields_b = faces(2, 6)
+    result = local_part(flux, jump)
+
+    up_hot, down_hot = one_hot(halo_key, neigh[0:1]), one_hot(halo_key, neigh[1:2])
+    up_copy.wait()
+    outer[0] = outer[0] + pick(up_in[...], up_hot, 2)
+    down_copy.wait()
+    outer[1] = outer[1] + pick(down_in[...], down_hot, 2)
+    inner_a, other_a, jump, fields_a = faces(0, 2)
+    result = result + halo_part_of(jump)
+    inner, other = Gas.merged(inner_a, inner_b), Gas.merged(other_a, other_b)
+    side, gap, inv_root, lam, lam_n, diff = stacked(fields_a, fields_b)
     weighted = []
     for v in range(5):
         residual = result[:, v * elements:(v + 1) * elements]
@@ -412,7 +453,6 @@
         weighted.append(residual * weight)
     stores[0].start()
 
-    asm_t = asm_t_ref[...].astype(BF16)
     back = [apply_table(asm_t, weighted[v]) for v in range(5)]
     grads = [gas.against([b[POINTS * j:POINTS * (j + 1)] for b in back]) for j in range(3)]
     face_back = [b[3 * POINTS:] for b in back]
@@ -428,7 +468,6 @@
         edge_grad.append([one[i] + two[i] for i in range(3)])
     first_grad, second_grad = cross(second, face_grad), cross(face_grad, first)
     smoothing = damping[:, 1:2]
-    geo_t = geo_t_ref[...].astype(BF16)
     stack = [
         jnp.concatenate(
             [edge_grad[0][i], edge_grad[1][i], edge_grad[2][i], first_grad[i], second_grad[i]], axis=0
@@ -459,14 +498,11 @@
     inner_dspeed, other_dspeed = inner.speed_change(face_n, size), other.speed_change(face_n, size)
     dlam = 0.5 * (inner_dspeed + other_dspeed) + gap * (inner_dspeed - other_dspeed) * inv_root
     inner_change, other_change = inner.along_change(face_n), other.along_change(face_n)
-    columns = []
+    jump = []
     for v in range(5):
         ddiff = other.du[v] - inner.du[v]
-        djump = 0.5 * (other_change[v] - inner_change[v] - dlam * diff[v] - lam * ddiff)
-        columns.append(
-            jnp.concatenate([flux_change[0][v], flux_change[1][v], flux_change[2][v], djump], axis=0)
-        )
-    result = apply_table(asm, jnp.concatenate(columns, axis=1))
+        jump.append(0.5 * (other_change[v] - inner_change[v] - dlam * diff[v] - lam * ddiff))
+    result = assembled(flux_change, jump)
     for v in range(5):
         change_ref[v] = result[:, v * elements:(v + 1) * elements]
     stores[1].start()
@@ -492,11 +528,10 @@
     dface = [one[i] + two[i] for i in range(3)]
     inner_dalong, other_dalong = inner.along(dface), other.along(dface)
     dlam_n = dot3(lam_n, dface)
-    columns = []
-    for v in range(5):
-        jump = 0.5 * (other_dalong[v] - inner_dalong[v] - dlam_n * diff[v])
-        columns.append(jnp.concatenate([dflux[0][v], dflux[1][v], dflux[2][v], jump], axis=0))
-    moved = apply_table(asm, jnp.concatenate(columns, axis=1))
+    jump = [
+        0.5 * (other_dalong[v] - inner_dalong[v] - dlam_n * diff[v]) for v in range(5)
+    ]
+    moved = assembled(dflux, jump)
     squares = jnp.sum(moved * moved, axis=0, keepdims=True)
     squares = sum(squares[:, v * elements:(v + 1) * elements] for v in range(5))
     curvature = squares * weight

time: 27.1 us -> 27 us (level)
  no operation moved by 1% of the time
where the time goes in v2:
time: 27 us; the launch traced here: 26.8 us
  Pallas kernels  26.2 us (97%)
  between operations  0.64 us (2%)
    pallas_call x1, Pallas kernels, body(): pl.pallas_call(functools.partial(kernel, n, group), out_shape=shapes, in_...  24.5 us
    pallas_call x1, Pallas kernels, body(): pl.pallas_call(write_out, out_shape=shapes, in_specs=[hbm] * 3, out_specs...  1.71 us

profile of v2, /device:TPU:0, one launch (start us, length us, event | category | flops | bytes accessed | tf_op | source)
XLA Modules:
  0.0 26.8 jit_solution(9680531834179537190)
XLA Ops:
  0.6 24.5 %shard_map.184 = (f32[5,64,64]{2,1,0:T(8,128)}, f32[5,64,64]{2,1,0:T(8,128)}, f32[3,102]{1,0:T(4,128)}) custom-call(f32[5,64,64]{2,1,0:T(8,128)} %refs_0_.1, f32[5,64,64]{2,1,0:T(8,128)} %refs_1_.1, f32[1,5]{1,0:T(1,128)} %bitcast.6, f32[3,102]{1,0:T(4,128)} %refs_3_.1, f32[1,2]{1,0:T(1,128)} %bitcast.7, s32[6,64]{1,0:T(8,128)} %refs_5_.1, s32[8,64]{1,0:T(8,128)} %refs_6_.1, ...), custom_call_target="tpu_custom_call" | custom-call | tf_op jit(solution)/shard_map/pallas_call | solution.py:604
  25.1 1.7 %shard_map.185 = (f32[5,64,64]{2,1,0:T(8,128)}, f32[5,64,64]{2,1,0:T(8,128)}, f32[3,102]{1,0:T(4,128)}) custom-call(f32[5,64,64]{2,1,0:T(8,128)} %get-tuple-element.6.refs_0_, f32[5,64,64]{2,1,0:T(8,128)} %get-tuple-element.7.refs_1_, f32[3,102]{1,0:T(4,128)} %get-tuple-element.8.refs_2_), custom_call_target="tpu_custom_call" | custom-call | tf_op jit(solution)/shard_map/pallas_call | solution.py:620

commit v3 on v2

--- a/solution.py
+++ b/solution.py
@@ -232,7 +232,7 @@
         pltpu.make_async_copy(source, results[i], load_sem.at[INPUTS + i])
         for i, source in enumerate((res_ref, change_ref, update_ref))
     ]
-    for i in LOAD_ORDER:
+    for i in LOAD_ORDER[:6]:
         loads[i].start()
     me = lax.axis_index("parts")
     right, left = lax.rem(me + 1, n), lax.rem(me + n - 1, n)
@@ -275,6 +275,9 @@
     barrier = pltpu.get_barrier_semaphore()
     for device in [left, right] + partners:
         pl.semaphore_signal(barrier, inc=1, device_id=(device,), device_id_type=MESH)
+
+    for i in LOAD_ORDER[6:]:
+        loads[i].start()
 
     for i in LOAD_ORDER[:6]:
         loads[i].wait()
@@ -363,9 +366,11 @@
     geo = geo_ref[...].astype(BF16)
 
     def edges_of(corners):
-        hi, mid, lo = split(jnp.concatenate(corners, axis=1), 3)
-        out = jnp.dot(geo, rows_of([hi, mid, lo, hi, mid, hi]), preferred_element_type=F32)
-        rows = [out[:, i * elements:(i + 1) * elements] for i in range(3)]
+        rows = []
+        for corner in corners:
+            hi, mid, lo = split(corner, 3)
+            data = rows_of([hi, mid, lo, hi, mid, hi])
+            rows.append(jnp.dot(geo, data, preferred_element_type=F32))
         volume = [[rows[i][POINTS * j:POINTS * (j + 1)] for i in range(3)] for j in range(3)]
         base = 3 * POINTS
         first = [rows[i][base:base + 6 * FACE] for i in range(3)]

time: 27 us -> 26.7 us (0.989)
  Pallas kernels: 26.2 us -> 25.9 us
    pallas_call x1, Pallas kernels: 24.5 us -> 24.2 us  [body(): pl.pallas_call(functools.partial(kernel, n, group), out_shape=shapes, in_...]
where the time goes in v3:
time: 26.7 us; the launch traced here: 26.5 us
  Pallas kernels  25.9 us (97%)
  between operations  0.64 us (2%)
    pallas_call x1, Pallas kernels, body(): pl.pallas_call(functools.partial(kernel, n, group), out_shape=shapes, in_...  24.2 us
    pallas_call x1, Pallas kernels, body(): pl.pallas_call(write_out, out_shape=shapes, in_specs=[hbm] * 3, out_specs...  1.71 us

profile of v3, /device:TPU:0, one launch (start us, length us, event | category | flops | bytes accessed | tf_op | source)
XLA Modules:
  0.0 26.5 jit_solution(17175259694504427954)
XLA Ops:
  0.6 24.2 %shard_map.184 = (f32[5,64,64]{2,1,0:T(8,128)}, f32[5,64,64]{2,1,0:T(8,128)}, f32[3,102]{1,0:T(4,128)}) custom-call(f32[5,64,64]{2,1,0:T(8,128)} %refs_0_.1, f32[5,64,64]{2,1,0:T(8,128)} %refs_1_.1, f32[1,5]{1,0:T(1,128)} %bitcast.6, f32[3,102]{1,0:T(4,128)} %refs_3_.1, f32[1,2]{1,0:T(1,128)} %bitcast.7, s32[6,64]{1,0:T(8,128)} %refs_5_.1, s32[8,64]{1,0:T(8,128)} %refs_6_.1, ...), custom_call_target="tpu_custom_call" | custom-call | tf_op jit(solution)/shard_map/pallas_call | solution.py:609
  24.8 1.7 %shard_map.185 = (f32[5,64,64]{2,1,0:T(8,128)}, f32[5,64,64]{2,1,0:T(8,128)}, f32[3,102]{1,0:T(4,128)}) custom-call(f32[5,64,64]{2,1,0:T(8,128)} %get-tuple-element.6.refs_0_, f32[5,64,64]{2,1,0:T(8,128)} %get-tuple-element.7.refs_1_, f32[3,102]{1,0:T(4,128)} %get-tuple-element.8.refs_2_), custom_call_target="tpu_custom_call" | custom-call | tf_op jit(solution)/shard_map/pallas_call | solution.py:625
